TPU v7x, 128 devices: a whole 4x4x4 slice. The times are simulated.
128 devices in a mesh: src: 8 (over z_lo, x), snk: 16 (over y, z_hi, core).
Axes of the slice: x: 4, y: 4, z: 4 (z_hi: 2, z_lo: 2; z = z_hi * 2 + z_lo), core: 2. Of those that a mesh axis runs over, the one named last changes fastest.
Arguments:
- perambulator: bfloat16 [8, 16, 2, 1024, 1024], P('src', 'snk'), may hold values from -0.25976562 to 0.25976562
- elementals: bfloat16 [16, 4, 2, 256, 256], P('snk', None, None, 'src'), may hold values from -0.25 to 0.25
- momentum: int32 [16], P('snk'), may hold values from 0 to 3
- routes: int32 [8, 16, 16, 1], P('src'), may hold values from 0 to 15; in each aligned block of 16 rows (0 to 15, 16 to 31, ..., all dimensions but the last counted through in order) at most 2 rows name the same one
- node_of: int32 [8, 16, 16], P('src'), may hold values from 0 to 15
- owner_slot: int32 [16], replicated, may hold values from 0 to 15, each once
Outputs:
- nodes: float32 [16, 2, 64, 1024], P('snk', None, 'src')
Inputs may be any that keep to these rules, and one draw needn't show every extreme that they name: `routes`: among the 16 slabs of one tile (one s and k), at most 2 name the same sink timeslice. `owner_slot`: each value appears exactly once.
All inputs are finite; a program needn't handle non-finite values.
Results may differ from a plain program's by a relative error of at most 0.005.
Values may be sent and summed in bfloat16 or wider, within the bound.
A program may use at most 128 MiB of HBM per device.

v0:
```python
import jax
import jax.numpy as jnp
from jax import lax
from jax.experimental import pallas as pl
from jax.experimental.pallas import tpu as pltpu
from jax.sharding import PartitionSpec as P

MESH = pl.DeviceIdType.MESH
F32 = jnp.float32
BF16 = jnp.bfloat16
PIECES = 4


def iota(shape, dim):
    return lax.broadcasted_iota(jnp.int32, shape, dim)


def dot(a, b):
    return jnp.dot(a, b, preferred_element_type=F32)


def dot_nt(a, b):
    return lax.dot_general(a, b, (((1,), (1,)), ((), ())), preferred_element_type=F32)


def kernel(
    momentum, owner_slot, elementals, routes, node_of, tile_hbm, out_ref,
    tile, phi, spread, kron, place, select, order, lane_order,
    sent, held, gathered, factor, kept, core_out, core_in,
    x_out, x_in, own_sum, y_out, y_in, z_out, z_in,
    tile_sem, phi_s, phi_r, ex_s, ex_r, core_s, core_r, x_s, x_r, y_s, y_r, z_s, z_r,
):
    source = lax.axis_index("src")
    sink = lax.axis_index("snk")
    zl, xx = source // 4, source % 4
    yy, zh, core = sink // 4, (sink // 2) % 2, sink % 2

    load = pltpu.make_async_copy(tile_hbm, tile, tile_sem)
    load.start()

    barrier = pltpu.get_barrier_semaphore()

    def greet_source(n, _):
        pl.semaphore_signal(barrier, inc=1, device_id=((source + n) % 8, sink), device_id_type=MESH)
        return 0

    def greet_sink(n, _):
        pl.semaphore_signal(barrier, inc=1, device_id=(source, (sink + n) % 16), device_id_type=MESH)
        return 0

    def at_z(zlo, zhi):
        return (zlo * 4 + xx, (yy * 2 + zhi) * 2 + core)

    lax.fori_loop(1, 8, greet_source, 0)
    lax.fori_loop(1, 16, greet_sink, 0)
    pl.semaphore_signal(barrier, inc=1, device_id=at_z(1 - zl, 1 - zh), device_id_type=MESH)

    phi[source] = elementals[momentum[0]]
    pl.semaphore_wait(barrier, 23)

    def phi_copy(n, owner):
        return pltpu.make_async_remote_copy(
            src_ref=phi.at[owner], dst_ref=phi.at[owner],
            send_sem=phi_s.at[n], recv_sem=phi_r.at[n],
            device_id=((source + n) % 8, sink), device_id_type=MESH,
        )

    def phi_start(n, _):
        phi_copy(n, source).start()
        return 0

    lax.fori_loop(1, 8, phi_start, 0)

    spread[...] = jnp.where(iota((256, 1024), 1) // 4 == iota((256, 1024), 0), 1.0, 0.0).astype(BF16)
    position = jnp.zeros((16, 16), jnp.int32)
    for node in range(16):
        position = position + jnp.where(node_of[...] == node, owner_slot[node], 0)
    code = routes[...] * 16 + (position % 2) * 8 + position // 2
    widen = jnp.where(iota((16, 256), 1) % 16 == iota((16, 256), 0), 1.0, 0.0).astype(BF16)
    wide = dot(code.astype(F32).astype(BF16), widen)
    wide = jnp.where(iota((16, 256), 1) // 16 == iota((16, 256), 0), wide, 0.0)
    named = jnp.sum(wide, axis=0, keepdims=True).astype(jnp.int32)
    select[...] = jnp.where(iota((256, 256), 0) == named, 1.0, 0.0).astype(BF16)
    row = iota((256, 256), 0)
    order[...] = jnp.where(iota((256, 256), 1) == (row % 16) * 16 + row // 16, 1.0, 0.0).astype(BF16)

    def phi_wait(n, _):
        copy = phi_copy(n, (source + 8 - n) % 8)
        copy.wait_recv()
        return 0

    lax.fori_loop(1, 8, phi_wait, 0)
    load.wait()

    low_lanes = iota((256, 128), 1) < 64

    def ex_copy(n, dest, origin):
        return pltpu.make_async_remote_copy(
            src_ref=sent.at[n, dest], dst_ref=held.at[n, origin],
            send_sem=ex_s.at[n, dest], recv_sem=ex_r.at[n, origin],
            device_id=(source, dest), device_id_type=MESH,
        )

    def dress(n, _):
        t = (xx + 1 + n) % 4
        rows = iota((256, 256), 0)
        il, b = rows // 16, rows % 16
        e = b * 16 + (il // 8) * 8 + t * 2 + (il % 8) // 4
        place[...] = jnp.where(iota((256, 256), 1) == e, 1.0, 0.0).astype(BF16)
        spins = iota((256, 1024), 1) % 4 == (iota((256, 1024), 0) // 16) % 4
        for part in range(2):
            whole = jnp.concatenate([phi[q, part] for q in range(8)], axis=0)
            placed = dot(place[...], whole).astype(BF16)
            grown = dot(placed, spread[...])
            kron[part * 256:(part + 1) * 256, :] = jnp.where(spins, grown, 0.0).astype(BF16)

        def columns(chip):
            lanes = pl.ds(pl.multiple_of(chip * 128, 128), 128)
            right = jnp.concatenate([tile[0, :, lanes], tile[1, :, lanes]], axis=1)
            both = dot(kron[...], right)
            real = both[:256, :128] - both[256:, 128:]
            imag = both[:256, 128:] + both[256:, :128]
            low = jnp.where(low_lanes, real, pltpu.roll(imag, 64, 1)).astype(BF16)
            high = jnp.where(low_lanes, pltpu.roll(real, 64, 1), imag).astype(BF16)
            return low, high

        def remote(h, _):
            chip = ((yy + h // 2 + 1) % 4) * 2 + (zh + h + 1) % 2
            low, high = columns(chip)
            sent[n, 2 * chip] = low
            sent[n, 2 * chip + 1] = high
            ex_copy(n, 2 * chip, sink).start()
            ex_copy(n, 2 * chip + 1, sink).start()
            return 0

        lax.fori_loop(0, 7, remote, 0)
        chip = yy * 2 + zh
        low, high = columns(chip)
        held[n, sink] = jnp.where(core == 0, low, high)
        sent[n, sink + 1 - 2 * core] = jnp.where(core == 0, high, low)
        ex_copy(n, sink + 1 - 2 * core, sink).start()
        return 0

    lax.fori_loop(0, PIECES, dress, 0)

    for t in range(4):
        r = iota((256, 1024), 0)
        target = (r % 16) * 64 + (r // 128) * 32 + t * 8 + (r // 16) % 8
        lane_order[t] = jnp.where(iota((256, 1024), 1) == target, 1.0, 0.0).astype(BF16)

    def core_copy(g):
        return pltpu.make_async_remote_copy(
            src_ref=core_out.at[g], dst_ref=core_in.at[g],
            send_sem=core_s.at[g], recv_sem=core_r.at[g],
            device_id=(source, sink + 1 - 2 * core), device_id_type=MESH,
        )

    def x_copy(ni, tj):
        return pltpu.make_async_remote_copy(
            src_ref=x_out.at[ni, tj], dst_ref=x_in.at[ni, tj],
            send_sem=x_s.at[ni, tj], recv_sem=x_r.at[ni, tj],
            device_id=(zl * 4 + (xx + 1 + ni) % 4, sink), device_id_type=MESH,
        )

    def settle(g, ni, nj):
        core_copy(g).wait_recv()
        total = kept[g] + core_in[g].astype(F32)
        tj = (xx + 1 + nj) % 4

        @pl.when(ni < 3)
        def _():
            x_out[ni, tj] = total.astype(BF16)
            x_copy(ni, tj).start()

        @pl.when(ni == 3)
        def _():
            own_sum[tj] = total

    def pair(n, g):
        ni = jnp.where(g <= n, n, g - n - 1)
        nj = jnp.where(g <= n, g, n)
        return ni, nj

    def piece(n, _):
        def arrive(o, _):
            origin = (sink + o) % 16
            ex_copy(n, sink, origin).wait_recv()
            return 0

        lax.fori_loop(1, 16, arrive, 0)

        def collect(pairing, _):
            first = pl.ds(pl.multiple_of(pairing * 32, 32), 16)
            second = pl.ds(pl.multiple_of(pairing * 32 + 16, 16), 16)
            left = held[n, :, first, :].reshape(256, 128)
            right = held[n, :, second, :].reshape(256, 128)
            sums = dot(select[...], jnp.concatenate([left, right], axis=1)).astype(BF16)
            for r in range(16):
                lanes = slice(r * 128, (r + 1) * 128)
                gathered[first, lanes] = sums[r * 16:(r + 1) * 16, :128]
                gathered[second, lanes] = sums[r * 16:(r + 1) * 16, 128:]
            return 0

        lax.fori_loop(0, 8, collect, 0)

        def arrange(r, _):
            lanes = pl.ds(pl.multiple_of(r * 128, 128), 128)
            plain = dot(order[...], gathered[:, lanes])
            turned = pltpu.roll(plain, 64, 1)
            turned = jnp.where(low_lanes, turned, -turned)
            both = jnp.stack([plain.reshape(32, 8, 128), turned.reshape(32, 8, 128)], axis=1)
            factor[n, :, lanes] = both.reshape(512, 128).astype(BF16)
            return 0

        lax.fori_loop(0, 16, arrange, 0)

        def block(g, _):
            ni, nj = pair(n, g)
            number = n * n + g
            right = jnp.concatenate([held[nj, r] for r in range(16)], axis=1)
            product = dot_nt(factor[ni], right)
            kept[number] = jnp.where(core == 0, product[:256], product[256:])
            core_out[number] = jnp.where(core == 0, product[256:], product[:256]).astype(BF16)
            core_copy(number).start()

            @pl.when(g > 0)
            def _():
                pi, pj = pair(n, g - 1)
                settle(number - 1, pi, pj)

            return 0

        lax.fori_loop(0, 2 * n + 1, block, 0)
        li, lj = pair(n, 2 * n)
        settle(n * n + 2 * n, li, lj)
        return 0

    lax.fori_loop(0, PIECES, piece, 0)

    def x_arrive(tj, total):
        summed = own_sum[tj]
        for ni in range(3):
            x_copy(ni, tj).wait_recv()
            summed = summed + x_in[ni, tj].astype(F32)
        return total + dot(summed.astype(BF16), lane_order[tj])

    whole = lax.fori_loop(0, 4, x_arrive, jnp.zeros((256, 1024), F32))
    y_out[...] = whole.reshape(4, 64, 1024).astype(BF16)

    def y_copy(n):
        return pltpu.make_async_remote_copy(
            src_ref=y_out.at[(yy + n) % 4], dst_ref=y_in.at[n - 1],
            send_sem=y_s.at[n - 1], recv_sem=y_r.at[n - 1],
            device_id=(source, ((yy + n) % 4) * 4 + zh * 2 + core), device_id_type=MESH,
        )

    for n in range(1, 4):
        y_copy(n).start()
    summed = y_out[yy].astype(F32)
    for n in range(1, 4):
        y_copy(n).wait_recv()
        summed = summed + y_in[n - 1].astype(F32)
    z_out[...] = summed.reshape(4, 16, 1024)

    def z_copy(n):
        z = zh * 2 + zl
        there = (z + n) % 4
        return pltpu.make_async_remote_copy(
            src_ref=z_out.at[there], dst_ref=z_in.at[n - 1],
            send_sem=z_s.at[n - 1], recv_sem=z_r.at[n - 1],
            device_id=at_z(there % 2, there // 2), device_id_type=MESH,
        )

    for n in range(1, 4):
        z_copy(n).start()
    final = z_out[zh * 2 + zl]
    for n in range(1, 4):
        z_copy(n).wait_recv()
        final = final + z_in[n - 1]
    out_ref[...] = final.reshape(2, 8, 1024)

    def phi_done(n, _):
        phi_copy(n, source).wait_send()
        return 0

    lax.fori_loop(1, 8, phi_done, 0)

    def ex_done(n, _):
        def one(o, _):
            ex_copy(n, (sink + o) % 16, sink).wait_send()
            return 0

        lax.fori_loop(1, 16, one, 0)
        return 0

    lax.fori_loop(0, PIECES, ex_done, 0)

    def core_done(g, _):
        core_copy(g).wait_send()
        return 0

    lax.fori_loop(0, 16, core_done, 0)

    def x_done(g, _):
        x_copy(g // 4, g % 4).wait_send()
        return 0

    lax.fori_loop(0, 12, x_done, 0)
    for n in range(1, 4):
        y_copy(n).wait_send()
        z_copy(n).wait_send()


def on_device(perambulator, elementals, momentum, routes, node_of, owner_slot):
    vmem = pl.BlockSpec(memory_space=pltpu.VMEM)
    smem = pl.BlockSpec(memory_space=pltpu.SMEM)
    dma = pltpu.SemaphoreType.DMA
    out = pl.pallas_call(
        kernel,
        out_shape=jax.ShapeDtypeStruct((2, 8, 1024), F32),
        in_specs=[smem, smem, vmem, vmem, vmem, pl.BlockSpec(memory_space=pl.ANY)],
        out_specs=vmem,
        scratch_shapes=[
            pltpu.VMEM((2, 1024, 1024), BF16),
            pltpu.VMEM((8, 2, 32, 256), BF16),
            pltpu.VMEM((256, 1024), BF16),
            pltpu.VMEM((512, 1024), BF16),
            pltpu.VMEM((256, 256), BF16),
            pltpu.VMEM((256, 256), BF16),
            pltpu.VMEM((256, 256), BF16),
            pltpu.VMEM((4, 256, 1024), BF16),
            pltpu.VMEM((4, 16, 256, 128), BF16),
            pltpu.VMEM((4, 16, 256, 128), BF16),
            pltpu.VMEM((256, 2048), BF16),
            pltpu.VMEM((4, 512, 2048), BF16),
            pltpu.VMEM((16, 256, 256), F32),
            pltpu.VMEM((16, 256, 256), BF16),
            pltpu.VMEM((16, 256, 256), BF16),
            pltpu.VMEM((3, 4, 256, 256), BF16),
            pltpu.VMEM((3, 4, 256, 256), BF16),
            pltpu.VMEM((4, 256, 256), F32),
            pltpu.VMEM((4, 64, 1024), BF16),
            pltpu.VMEM((3, 64, 1024), BF16),
            pltpu.VMEM((4, 16, 1024), F32),
            pltpu.VMEM((3, 16, 1024), F32),
            dma, dma((8,)), dma((8,)), dma((4, 16)), dma((4, 16)),
            dma((16,)), dma((16,)), dma((3, 4)), dma((3, 4)),
            dma((3,)), dma((3,)), dma((3,)), dma((3,)),
        ],
        compiler_params=pltpu.CompilerParams(
            collective_id=0, has_side_effects=True, vmem_limit_bytes=60 * 2**20
        ),
        cost_estimate=pl.CostEstimate(flops=20 * 10**9, bytes_accessed=8 * 2**20, transcendentals=0),
    )(
        momentum,
        owner_slot,
        elementals[0],
        routes[0, :, :, 0],
        node_of[0],
        perambulator[0, 0],
    )
    return out[None]


def solution(mesh):
    placed = (
        P("src", "snk", None, None, None),
        P("snk", None, None, "src", None),
        P("snk"),
        P("src", None, None, None),
        P("src", None, None),
        P(),
    )
    return jax.shard_map(
        on_device,
        mesh=mesh,
        in_specs=placed,
        out_specs=P("snk", None, "src", None),
        check_vma=False,
    )
```

profile of v0, /device:TPU:1, one launch (start us, length us, event | category | flops | bytes accessed | tf_op | source)
XLA Modules:
  0.0 109.8 jit_solution(4533628236638364456)
XLA Ops:
  0.7 107.6 %shard_map.64 = f32[2,8,1024]{2,1,0:T(8,128)} custom-call(s32[1]{0:T(128)S(6)} %copy.8.momentum, s32[16]{0:T(128)} %owner_slot.1, bf16[4,2,32,256]{3,2,1,0:T(8,128)(2,1)} %bitcast.7, s32[16,16]{1,0:T(8,128)} %bitcast.8, s32[16,16]{1,0:T(8,128)} %bitcast.9, bf16[2,1024,1024]{2,1,0:T(8,128)(2,1)} %bitcast.6), custom_call_target="tpu_custom_call" | custom-call | flops 20000000000 | bytes 8388608 | tf_op jit(solution)/shard_map/pallas_call | solution.py:318
  108.3 1.5 %copy.9 = f32[1,2,8,1024]{3,2,1,0:T(8,128)} copy(f32[1,2,8,1024]{3,2,1,0:T(8,128)} %bitcast.5) | data formatting | bytes 131072
where the time goes:
time: 111 us; the launch traced here: 110 us
  Pallas kernels  108 us (97%)
  local copies, waits for them, and re-layouts  1.47 us (1%)
    pallas_call x1, Pallas kernels, on_device(): pl.pallas_call(kernel, out_shape=jax.ShapeDtypeStruct((2, 8, 1024), F32),...  108 us

commit v1 on v0

v1 whole, which is shorter than its diff:
```python
import jax
import jax.numpy as jnp
from jax import lax
from jax.experimental import pallas as pl
from jax.experimental.pallas import tpu as pltpu
from jax.sharding import PartitionSpec as P

MESH = pl.DeviceIdType.MESH
F32 = jnp.float32
BF16 = jnp.bfloat16
PIECES = 4
STEPS_Y = sum(dy << (2 * h) for h, dy in enumerate((2, 1, 1, 3, 3, 2, 0)))


def iota(shape, dim):
    return lax.broadcasted_iota(jnp.int32, shape, dim)


def dot(a, b):
    return jnp.dot(a, b, preferred_element_type=F32)


def dot_nt(a, b):
    return lax.dot_general(a, b, (((1,), (1,)), ((), ())), preferred_element_type=F32)


def kernel(
    momentum, owner_slot, elementals, routes, node_of, tile_hbm, out_ref,
    tile, right, phi, placed, select, rows_order, lane_order,
    sent, held, factor, kept, core_out, core_in,
    x_out, x_in, own_sum, last_out, last_in,
    tile_sem, phi_s, phi_r, ex_s, ex_r, core_s, core_r, x_s, x_r, last_s, last_r,
):
    source = lax.axis_index("src")
    sink = lax.axis_index("snk")
    zl, xx = source // 4, source % 4
    yy, zh, core = sink // 4, (sink // 2) % 2, sink % 2

    load = pltpu.make_async_copy(tile_hbm, tile, tile_sem)
    load.start()

    barrier = pltpu.get_barrier_semaphore()

    def greet(there):
        pl.semaphore_signal(barrier, inc=1, device_id=there, device_id_type=MESH)

    def greet_source(n, _):
        greet(((source + n) % 8, sink))
        return 0

    def greet_sink(n, _):
        greet((source, (sink + n) % 16))
        return 0

    def greet_other(n, _):
        greet(((source + 4) % 8, (sink + 2 * n) % 16))
        return 0

    lax.fori_loop(1, 8, greet_source, 0)
    lax.fori_loop(1, 16, greet_sink, 0)
    lax.fori_loop(1, 8, greet_other, 0)

    phi[source] = elementals[momentum[0]]
    pl.semaphore_wait(barrier, 29)

    def phi_copy(n, owner):
        return pltpu.make_async_remote_copy(
            src_ref=phi.at[owner], dst_ref=phi.at[owner],
            send_sem=phi_s.at[n], recv_sem=phi_r.at[n],
            device_id=((source + n) % 8, sink), device_id_type=MESH,
        )

    def phi_start(n, _):
        phi_copy(n, source).start()
        return 0

    lax.fori_loop(1, 8, phi_start, 0)

    row, col = iota((256, 256), 0), iota((256, 256), 1)

    spins = jnp.where(col == (row & 63) * 4 + (row >> 6), 1.0, 0.0).astype(BF16)
    load.wait()

    def by_spin(chip, _):
        lanes = pl.ds(pl.multiple_of(chip * 128, 128), 128)
        for part in range(4):
            rows = slice(part * 256, (part + 1) * 256)
            both = jnp.concatenate([tile[0, rows, lanes], tile[1, rows, lanes]], axis=1)
            sorted_rows = dot(spins, both).astype(BF16)
            for a in range(4):
                right[chip, a, part * 64:(part + 1) * 64] = sorted_rows[a * 64:(a + 1) * 64]
        return 0

    lax.fori_loop(0, 8, by_spin, 0)

    t = (xx + 1 + (row >> 6)) & 3
    wanted = (row & 15) * 16 + ((row >> 5) & 1) * 8 + t * 2 + ((row >> 4) & 1)
    place = jnp.where(col == wanted, 1.0, 0.0).astype(BF16)

    def phi_wait(n, _):
        phi_copy(n, (source + 8 - n) % 8).wait_recv()
        return 0

    lax.fori_loop(1, 8, phi_wait, 0)
    for part in range(2):
        whole = jnp.concatenate([phi[q, part] for q in range(8)], axis=0)
        placed[part * 256:(part + 1) * 256, :] = dot(place, whole).astype(BF16)

    low_lanes = iota((256, 128), 1) < 64

    def ex_copy(n, dest, origin):
        return pltpu.make_async_remote_copy(
            src_ref=sent.at[n, dest], dst_ref=held.at[n, origin],
            send_sem=ex_s.at[n, dest], recv_sem=ex_r.at[n, origin],
            device_id=(source, dest), device_id_type=MESH,
        )

    def chip_at(h):
        dy = (STEPS_Y >> (2 * h)) & 3
        return ((yy + dy) % 4) * 2 + (zh + h + 1) % 2

    def columns(chip, a):
        both = dot(placed[...], right[chip, a])
        real = both[:256, :128] - both[256:, 128:]
        imag = both[:256, 128:] + both[256:, :128]
        low = jnp.where(low_lanes, real, pltpu.roll(imag, 64, 1)).astype(BF16)
        high = jnp.where(low_lanes, pltpu.roll(real, 64, 1), imag).astype(BF16)
        return low, high

    def dress(h, _):
        chip = chip_at(h)
        for a in range(4):
            low, high = columns(chip, a)
            for n in range(PIECES):
                sent[n, 2 * chip, a * 64:(a + 1) * 64] = low[n * 64:(n + 1) * 64]
                sent[n, 2 * chip + 1, a * 64:(a + 1) * 64] = high[n * 64:(n + 1) * 64]
        ex_copy(0, 2 * chip, sink).start()
        ex_copy(0, 2 * chip + 1, sink).start()
        return 0

    lax.fori_loop(0, 7, dress, 0)
    partner = sink + 1 - 2 * core
    for a in range(4):
        low, high = columns(yy * 2 + zh, a)
        mine = jnp.where(core == 0, low, high)
        theirs = jnp.where(core == 0, high, low)
        for n in range(PIECES):
            held[n, sink, a * 64:(a + 1) * 64] = mine[n * 64:(n + 1) * 64]
            sent[n, partner, a * 64:(a + 1) * 64] = theirs[n * 64:(n + 1) * 64]
    ex_copy(0, partner, sink).start()

    def send(n, _):
        def one(h, _):
            ex_copy(n, 2 * chip_at(h % 7) + h // 7, sink).start()
            return 0

        lax.fori_loop(0, 14, one, 0)
        ex_copy(n, partner, sink).start()
        return 0

    lax.fori_loop(1, PIECES, send, 0)

    position = jnp.zeros((16, 16), jnp.int32)
    for node in range(16):
        position = position + jnp.where(node_of[...] == node, owner_slot[node], 0)
    code = routes[...] * 16 + (position & 1) * 8 + (position >> 1)
    slab_row, slab_lane = iota((16, 256), 0), iota((16, 256), 1)
    widen = jnp.where((slab_lane & 15) == slab_row, 1.0, 0.0).astype(BF16)
    wide = dot(code.astype(F32).astype(BF16), widen)
    wide = jnp.where((slab_lane >> 4) == slab_row, wide, 0.0)
    named = jnp.sum(wide, axis=0, keepdims=True).astype(jnp.int32)
    select[...] = jnp.where(row == named, 1.0, 0.0).astype(BF16)

    spin, z_low, half, part, y_zh = row & 3, (row >> 4) & 1, (row >> 2) & 1, (row >> 3) & 1, row >> 5
    came = (spin << 6) | (z_low << 5) | (half << 4) | (part << 3) | y_zh
    rows_order[...] = jnp.where(col == came, 1.0, 0.0).astype(BF16)
    r, lane = iota((256, 1024), 0), iota((256, 1024), 1)
    target = (r & 15) * 64 + ((r >> 5) & 1) * 32 + ((r >> 4) & 1) * 4 + (r >> 6)
    for t in range(4):
        lane_order[t * 256:(t + 1) * 256] = jnp.where(lane == target + t * 8, 1.0, 0.0).astype(BF16)

    def core_copy(g):
        return pltpu.make_async_remote_copy(
            src_ref=core_out.at[g], dst_ref=core_in.at[g],
            send_sem=core_s.at[g], recv_sem=core_r.at[g],
            device_id=(source, partner), device_id_type=MESH,
        )

    def x_copy(ni, tj):
        return pltpu.make_async_remote_copy(
            src_ref=x_out.at[ni, tj], dst_ref=x_in.at[ni, tj],
            send_sem=x_s.at[ni, tj], recv_sem=x_r.at[ni, tj],
            device_id=(zl * 4 + (xx + 1 + ni) % 4, sink), device_id_type=MESH,
        )

    def settle(g, ni, nj):
        core_copy(g).wait_recv()
        total = kept[g] + core_in[g].astype(F32)
        tj = (xx + 1 + nj) % 4

        @pl.when(ni < 3)
        def _():
            x_out[ni, tj] = total.astype(BF16)
            x_copy(ni, tj).start()

        @pl.when(ni == 3)
        def _():
            own_sum[tj] = total

    def block(number, ni, nj):
        side = jnp.concatenate([held[nj, r] for r in range(16)], axis=1)
        product = dot_nt(factor[ni], side)
        kept[number] = jnp.where(core == 0, product[:256], product[256:])
        core_out[number] = jnp.where(core == 0, product[256:], product[:256]).astype(BF16)
        core_copy(number).start()

    def piece(n, _):
        def arrive(o, _):
            ex_copy(n, sink, (sink + o) % 16).wait_recv()
            return 0

        lax.fori_loop(1, 16, arrive, 0)

        def earlier(m, _):
            number = n * n + m
            block(number, m, n)
            pi = jnp.where(m == 0, n - 1, m - 1)
            pj = jnp.where(m == 0, n - 1, n)
            settle(number - 1, pi, pj)
            return 0

        lax.fori_loop(0, n, earlier, 0)

        def collect(pairing, _):
            first = pl.ds(pl.multiple_of(pairing * 32, 32), 16)
            second = pl.ds(pl.multiple_of(pairing * 32 + 16, 16), 16)
            pair = [held[n, :, first, :].reshape(256, 128), held[n, :, second, :].reshape(256, 128)]
            sums = dot(select[...], jnp.concatenate(pair, axis=1))
            for k in range(2):
                plain = sums[:, k * 128:(k + 1) * 128]
                turned = pltpu.roll(plain, 64, 1)
                turned = jnp.where(low_lanes, turned, -turned)
                both = jnp.stack([plain.reshape(32, 8, 128), turned.reshape(32, 8, 128)], axis=1).astype(BF16)
                for r in range(16):
                    for c in range(2):
                        rows = pl.ds(pl.multiple_of(c * 256 + pairing * 32 + k * 16, 16), 16)
                        factor[n, rows, r * 128:(r + 1) * 128] = both[2 * r + c].reshape(16, 128)
            return 0

        lax.fori_loop(0, 8, collect, 0)

        def later(m, _):
            number = n * n + n + m
            block(number, n, m)

            @pl.when(number > 0)
            def _():
                pi = jnp.where(m == 0, n - 1, n)
                pj = jnp.where(m == 0, n, m - 1)
                settle(number - 1, pi, pj)

            return 0

        lax.fori_loop(0, n + 1, later, 0)
        return 0

    lax.fori_loop(0, PIECES, piece, 0)
    settle(15, 3, 3)

    arrived = []
    for tj in range(4):
        summed = own_sum[tj]
        for ni in range(3):
            x_copy(ni, tj).wait_recv()
            summed = summed + x_in[ni, tj].astype(F32)
        arrived.append(dot(rows_order[...], summed.astype(BF16)).astype(BF16))
    whole = dot(jnp.concatenate(arrived, axis=1), lane_order[...])
    last_out[...] = whole.reshape(16, 16, 1024).astype(BF16)

    mine = yy * 4 + zh * 2 + zl

    def last_copy(n):
        there = (mine + n) % 16
        return pltpu.make_async_remote_copy(
            src_ref=last_out.at[there], dst_ref=last_in.at[n],
            send_sem=last_s.at[n], recv_sem=last_r.at[n],
            device_id=((there % 2) * 4 + xx, (there // 2) * 2 + core), device_id_type=MESH,
        )

    def last_start(n, _):
        last_copy(n).start()
        return 0

    lax.fori_loop(1, 16, last_start, 0)

    def last_sum(n, total):
        last_copy(n).wait_recv()
        return total + last_in[n].astype(F32)

    final = lax.fori_loop(1, 16, last_sum, last_out[mine].astype(F32))
    out_ref[...] = final.reshape(2, 8, 1024)

    def phi_done(n, _):
        phi_copy(n, source).wait_send()
        return 0

    lax.fori_loop(1, 8, phi_done, 0)

    def ex_done(n, _):
        def one(o, _):
            ex_copy(n, (sink + o) % 16, sink).wait_send()
            return 0

        lax.fori_loop(1, 16, one, 0)
        return 0

    lax.fori_loop(0, PIECES, ex_done, 0)

    def core_done(g, _):
        core_copy(g).wait_send()
        return 0

    lax.fori_loop(0, 16, core_done, 0)

    def x_done(g, _):
        x_copy(g // 4, g % 4).wait_send()
        return 0

    lax.fori_loop(0, 12, x_done, 0)

    def last_done(n, _):
        last_copy(n).wait_send()
        return 0

    lax.fori_loop(1, 16, last_done, 0)


def on_device(perambulator, elementals, momentum, routes, node_of, owner_slot):
    vmem = pl.BlockSpec(memory_space=pltpu.VMEM)
    smem = pl.BlockSpec(memory_space=pltpu.SMEM)
    dma = pltpu.SemaphoreType.DMA
    out = pl.pallas_call(
        kernel,
        out_shape=jax.ShapeDtypeStruct((2, 8, 1024), F32),
        in_specs=[smem, smem, vmem, vmem, vmem, pl.BlockSpec(memory_space=pl.ANY)],
        out_specs=vmem,
        scratch_shapes=[
            pltpu.VMEM((2, 1024, 1024), BF16),
            pltpu.VMEM((8, 4, 256, 256), BF16),
            pltpu.VMEM((8, 2, 32, 256), BF16),
            pltpu.VMEM((512, 256), BF16),
            pltpu.VMEM((256, 256), BF16),
            pltpu.VMEM((256, 256), BF16),
            pltpu.VMEM((1024, 1024), BF16),
            pltpu.VMEM((4, 16, 256, 128), BF16),
            pltpu.VMEM((4, 16, 256, 128), BF16),
            pltpu.VMEM((4, 512, 2048), BF16),
            pltpu.VMEM((16, 256, 256), F32),
            pltpu.VMEM((16, 256, 256), BF16),
            pltpu.VMEM((16, 256, 256), BF16),
            pltpu.VMEM((3, 4, 256, 256), BF16),
            pltpu.VMEM((3, 4, 256, 256), BF16),
            pltpu.VMEM((4, 256, 256), F32),
            pltpu.VMEM((16, 16, 1024), BF16),
            pltpu.VMEM((16, 16, 1024), BF16),
            dma, dma((8,)), dma((8,)), dma((4, 16)), dma((4, 16)),
            dma((16,)), dma((16,)), dma((3, 4)), dma((3, 4)),
            dma((16,)), dma((16,)),
        ],
        compiler_params=pltpu.CompilerParams(
            collective_id=0, has_side_effects=True, vmem_limit_bytes=60 * 2**20
        ),
        cost_estimate=pl.CostEstimate(flops=20 * 10**9, bytes_accessed=8 * 2**20, transcendentals=0),
    )(
        momentum,
        owner_slot,
        elementals[0],
        routes[0, :, :, 0],
        node_of[0],
        perambulator[0, 0],
    )
    return out[None]


def solution(mesh):
    placed = (
        P("src", "snk", None, None, None),
        P("snk", None, None, "src", None),
        P("snk"),
        P("src", None, None, None),
        P("src", None, None),
        P(),
    )
    return jax.shard_map(
        on_device,
        mesh=mesh,
        in_specs=placed,
        out_specs=P("snk", None, "src", None),
        check_vma=False,
    )
```

time: 111 us -> 96.8 us (0.87)
  Pallas kernels: 108 us -> 93 us
    pallas_call x1, Pallas kernels: 108 us -> 93 us  [on_device(): pl.pallas_call(kernel, out_shape=jax.ShapeDtypeStruct((2, 8, 1024), F32),...]
where the time goes in v1:
time: 96.8 us; the launch traced here: 95.1 us
  Pallas kernels  93 us (96%)
  local copies, waits for them, and re-layouts  1.47 us (2%)
    pallas_call x1, Pallas kernels, on_device(): pl.pallas_call(kernel, out_shape=jax.ShapeDtypeStruct((2, 8, 1024), F32),...  93 us

profile of v1, /device:TPU:1, one launch (start us, length us, event | category | flops | bytes accessed | tf_op | source)
XLA Modules:
  0.0 95.1 jit_solution(2281304807851264218)
XLA Ops:
  0.7 93.0 %shard_map.64 = f32[2,8,1024]{2,1,0:T(8,128)} custom-call(s32[1]{0:T(128)S(6)} %copy.8.momentum, s32[16]{0:T(128)} %owner_slot.1, bf16[4,2,32,256]{3,2,1,0:T(8,128)(2,1)} %bitcast.7, s32[16,16]{1,0:T(8,128)} %bitcast.8, s32[16,16]{1,0:T(8,128)} %bitcast.9, bf16[2,1024,1024]{2,1,0:T(8,128)(2,1)} %bitcast.6), custom_call_target="tpu_custom_call" | custom-call | flops 20000000000 | bytes 8388608 | tf_op jit(solution)/shard_map/pallas_call | solution.py:342
  93.6 1.5 %copy.9 = f32[1,2,8,1024]{3,2,1,0:T(8,128)} copy(f32[1,2,8,1024]{3,2,1,0:T(8,128)} %bitcast.5) | data formatting | bytes 131072

commit v2 on v1

--- a/solution.py
+++ b/solution.py
@@ -9,8 +9,23 @@
 F32 = jnp.float32
 BF16 = jnp.bfloat16
 PIECES = 4
-STEPS_Y = sum(dy << (2 * h) for h, dy in enumerate((2, 1, 1, 3, 3, 2, 0)))
-
+WINDOW = 24
+
+
+def packed(values, bits):
+    return sum(value << (bits * n) for n, value in enumerate(values))
+
+
+CHIPS = ((0, 1), (1, 1), (1, 0), (2, 1), (3, 1), (2, 0), (3, 0))
+CHIPS_Y = packed([c[0] for c in CHIPS], 2)
+CHIPS_Z = packed([c[1] for c in CHIPS], 1)
+PEERS = (
+    (0, 1, 0), (1, 1, 0), (1, 0, 0), (2, 1, 0), (3, 1, 0), (2, 0, 0), (0, 1, 1), (1, 1, 1),
+    (3, 0, 0), (2, 1, 1), (3, 1, 1), (1, 0, 1), (2, 0, 1), (3, 0, 1), (0, 0, 1),
+)
+PEERS_Y = packed([p[0] for p in PEERS], 2)
+PEERS_Z = packed([p[1] for p in PEERS], 1)
+PEERS_C = packed([p[2] for p in PEERS], 1)
 
 def iota(shape, dim):
     return lax.broadcasted_iota(jnp.int32, shape, dim)
@@ -60,28 +75,21 @@
     lax.fori_loop(1, 16, greet_sink, 0)
     lax.fori_loop(1, 8, greet_other, 0)
 
+    row, col = iota((256, 256), 0), iota((256, 256), 1)
     phi[source] = elementals[momentum[0]]
-    pl.semaphore_wait(barrier, 29)
-
-    def phi_copy(n, owner):
-        return pltpu.make_async_remote_copy(
-            src_ref=phi.at[owner], dst_ref=phi.at[owner],
-            send_sem=phi_s.at[n], recv_sem=phi_r.at[n],
-            device_id=((source + n) % 8, sink), device_id_type=MESH,
-        )
-
-    def phi_start(n, _):
-        phi_copy(n, source).start()
-        return 0
-
-    lax.fori_loop(1, 8, phi_start, 0)
-
-    row, col = iota((256, 256), 0), iota((256, 256), 1)
+
+    def chip_at(h):
+        dy, dz = (CHIPS_Y >> (2 * h)) & 3, (CHIPS_Z >> h) & 1
+        return ((yy + dy) % 4) * 2 + (zh + dz) % 2
+
+    def peer_at(j):
+        dy, dz, dc = (PEERS_Y >> (2 * j)) & 3, (PEERS_Z >> j) & 1, (PEERS_C >> j) & 1
+        return ((yy + dy) % 4) * 4 + ((zh + dz) % 2) * 2 + (core + dc) % 2
 
     spins = jnp.where(col == (row & 63) * 4 + (row >> 6), 1.0, 0.0).astype(BF16)
-    load.wait()
-
-    def by_spin(chip, _):
+
+    def by_spin(h, _):
+        chip = chip_at(h)
         lanes = pl.ds(pl.multiple_of(chip * 128, 128), 128)
         for part in range(4):
             rows = slice(part * 256, (part + 1) * 256)
@@ -91,6 +99,22 @@
                 right[chip, a, part * 64:(part + 1) * 64] = sorted_rows[a * 64:(a + 1) * 64]
         return 0
 
+
+    pl.semaphore_wait(barrier, 29)
+
+    def phi_copy(n, owner):
+        return pltpu.make_async_remote_copy(
+            src_ref=phi.at[owner], dst_ref=phi.at[owner],
+            send_sem=phi_s.at[n], recv_sem=phi_r.at[n],
+            device_id=((source + n) % 8, sink), device_id_type=MESH,
+        )
+
+    def phi_start(n, _):
+        phi_copy(n, source).start()
+        return 0
+
+    lax.fori_loop(1, 8, phi_start, 0)
+    load.wait()
     lax.fori_loop(0, 8, by_spin, 0)
 
     t = (xx + 1 + (row >> 6)) & 3
@@ -114,10 +138,6 @@
             send_sem=ex_s.at[n, dest], recv_sem=ex_r.at[n, origin],
             device_id=(source, dest), device_id_type=MESH,
         )
-
-    def chip_at(h):
-        dy = (STEPS_Y >> (2 * h)) & 3
-        return ((yy + dy) % 4) * 2 + (zh + h + 1) % 2
 
     def columns(chip, a):
         both = dot(placed[...], right[chip, a])
@@ -149,16 +169,14 @@
             sent[n, partner, a * 64:(a + 1) * 64] = theirs[n * 64:(n + 1) * 64]
     ex_copy(0, partner, sink).start()
 
-    def send(n, _):
-        def one(h, _):
-            ex_copy(n, 2 * chip_at(h % 7) + h // 7, sink).start()
-            return 0
-
-        lax.fori_loop(0, 14, one, 0)
-        ex_copy(n, partner, sink).start()
-        return 0
-
-    lax.fori_loop(1, PIECES, send, 0)
+    def ex_send(q):
+        return ex_copy(q // 15, peer_at(q % 15), sink)
+
+    def ex_start(q, _):
+        ex_send(q).start()
+        return 0
+
+    lax.fori_loop(15, WINDOW, ex_start, 0)
 
     position = jnp.zeros((16, 16), jnp.int32)
     for node in range(16):
@@ -176,8 +194,9 @@
     rows_order[...] = jnp.where(col == came, 1.0, 0.0).astype(BF16)
     r, lane = iota((256, 1024), 0), iota((256, 1024), 1)
     target = (r & 15) * 64 + ((r >> 5) & 1) * 32 + ((r >> 4) & 1) * 4 + (r >> 6)
-    for t in range(4):
-        lane_order[t * 256:(t + 1) * 256] = jnp.where(lane == target + t * 8, 1.0, 0.0).astype(BF16)
+    for m in range(4):
+        t = (xx + 4 - m) % 4
+        lane_order[m * 256:(m + 1) * 256] = jnp.where(lane == target + t * 8, 1.0, 0.0).astype(BF16)
 
     def core_copy(g):
         return pltpu.make_async_remote_copy(
@@ -210,27 +229,37 @@
     def block(number, ni, nj):
         side = jnp.concatenate([held[nj, r] for r in range(16)], axis=1)
         product = dot_nt(factor[ni], side)
-        kept[number] = jnp.where(core == 0, product[:256], product[256:])
-        core_out[number] = jnp.where(core == 0, product[256:], product[:256]).astype(BF16)
+        kept[number] = product[:256]
+        core_out[number] = product[256:].astype(BF16)
         core_copy(number).start()
 
-    def piece(n, _):
-        def arrive(o, _):
+    def arrive(n):
+        def one(o, _):
             ex_copy(n, sink, (sink + o) % 16).wait_recv()
+            q = n * 15 + o - 1 + WINDOW
+
+            @pl.when(q < 15 * PIECES)
+            def _():
+                ex_send(q - WINDOW).wait_send()
+                ex_send(q).start()
+
             return 0
 
-        lax.fori_loop(1, 16, arrive, 0)
-
+        lax.fori_loop(1, 16, one, 0)
+
+    def earlier_blocks(n, base):
         def earlier(m, _):
-            number = n * n + m
-            block(number, m, n)
-            pi = jnp.where(m == 0, n - 1, m - 1)
-            pj = jnp.where(m == 0, n - 1, n)
-            settle(number - 1, pi, pj)
+            block(base + m, m, n)
+
+            @pl.when(m > 0)
+            def _():
+                settle(base + m - 1, m - 1, n)
+
             return 0
 
         lax.fori_loop(0, n, earlier, 0)
 
+    def collect_piece(n, halfway=None):
         def collect(pairing, _):
             first = pl.ds(pl.multiple_of(pairing * 32, 32), 16)
             second = pl.ds(pl.multiple_of(pairing * 32 + 16, 16), 16)
@@ -243,61 +272,89 @@
                 both = jnp.stack([plain.reshape(32, 8, 128), turned.reshape(32, 8, 128)], axis=1).astype(BF16)
                 for r in range(16):
                     for c in range(2):
-                        rows = pl.ds(pl.multiple_of(c * 256 + pairing * 32 + k * 16, 16), 16)
+                        rows = pl.ds(pl.multiple_of(((core + c) % 2) * 256 + pairing * 32 + k * 16, 16), 16)
                         factor[n, rows, r * 128:(r + 1) * 128] = both[2 * r + c].reshape(16, 128)
             return 0
 
-        lax.fori_loop(0, 8, collect, 0)
-
+        lax.fori_loop(0, 4, collect, 0)
+        if halfway:
+            halfway()
+        lax.fori_loop(4, 8, collect, 0)
+
+    def later_blocks(n, base, start, stop):
         def later(m, _):
-            number = n * n + n + m
-            block(number, n, m)
-
-            @pl.when(number > 0)
+            block(base + m, n, n - m)
+
+            @pl.when(m > 0)
             def _():
-                pi = jnp.where(m == 0, n - 1, n)
-                pj = jnp.where(m == 0, n, m - 1)
-                settle(number - 1, pi, pj)
+                settle(base + m - 1, n, n - m + 1)
 
             return 0
 
-        lax.fori_loop(0, n + 1, later, 0)
-        return 0
-
-    lax.fori_loop(0, PIECES, piece, 0)
-    settle(15, 3, 3)
-
-    arrived = []
-    for tj in range(4):
-        summed = own_sum[tj]
-        for ni in range(3):
-            x_copy(ni, tj).wait_recv()
-            summed = summed + x_in[ni, tj].astype(F32)
-        arrived.append(dot(rows_order[...], summed.astype(BF16)).astype(BF16))
-    whole = dot(jnp.concatenate(arrived, axis=1), lane_order[...])
-    last_out[...] = whole.reshape(16, 16, 1024).astype(BF16)
-
-    mine = yy * 4 + zh * 2 + zl
-
-    def last_copy(n):
+        lax.fori_loop(start, stop, later, 0)
+
+    def last_copy(side, n):
         there = (mine + n) % 16
         return pltpu.make_async_remote_copy(
-            src_ref=last_out.at[there], dst_ref=last_in.at[n],
-            send_sem=last_s.at[n], recv_sem=last_r.at[n],
+            src_ref=last_out.at[side, there], dst_ref=last_in.at[side, n],
+            send_sem=last_s.at[side, n], recv_sem=last_r.at[side, n],
             device_id=((there % 2) * 4 + xx, (there // 2) * 2 + core), device_id_type=MESH,
         )
 
-    def last_start(n, _):
-        last_copy(n).start()
-        return 0
-
-    lax.fori_loop(1, 16, last_start, 0)
-
-    def last_sum(n, total):
-        last_copy(n).wait_recv()
-        return total + last_in[n].astype(F32)
-
-    final = lax.fori_loop(1, 16, last_sum, last_out[mine].astype(F32))
+    def sum_x(side):
+        for k in range(2):
+            tj = (xx + 4 - 2 * side - k) % 4
+            summed = own_sum[tj]
+            for ni in range(3):
+                x_copy(ni, tj).wait_recv()
+                summed = summed + x_in[ni, tj].astype(F32)
+            ordered = dot(rows_order[...], summed.astype(BF16)).astype(BF16)
+            last_out[side, :, :, k * 256:(k + 1) * 256] = ordered.reshape(16, 16, 256)
+
+        def last_start(n, _):
+            last_copy(side, n).start()
+            return 0
+
+        lax.fori_loop(1, 16, last_start, 0)
+
+    def sum_yz(side):
+        def last_sum(n, total):
+            last_copy(side, n).wait_recv()
+            return total + last_in[side, n].astype(F32)
+
+        total = lax.fori_loop(1, 16, last_sum, last_out[side, mine].astype(F32))
+        high = total.astype(BF16)
+        rest = total - high.astype(F32)
+        middle = rest.astype(BF16)
+        low = (rest - middle.astype(F32)).astype(BF16)
+        parts = dot(jnp.concatenate([high, middle, low], axis=0), lane_order[side * 512:(side + 1) * 512])
+        return (parts[:16] + parts[16:32]) + parts[32:]
+
+    mine = yy * 4 + zh * 2 + zl
+
+    def piece(n, _):
+        arrive(n)
+        collect_piece(n)
+        later_blocks(n, n * n, 0, n + 1)
+        earlier_blocks(n, n * n + n + 1)
+        settle(n * n + n, n, 0)
+
+        @pl.when(n > 0)
+        def _():
+            settle(n * n + 2 * n, n - 1, n)
+
+        return 0
+
+    lax.fori_loop(0, 3, piece, 0)
+    arrive(3)
+    earlier_blocks(3, 9)
+    collect_piece(3, lambda: settle(11, 2, 3))
+    later_blocks(3, 12, 0, 3)
+    sum_x(0)
+    later_blocks(3, 12, 3, 4)
+    settle(15, 3, 0)
+    sum_x(1)
+    final = sum_yz(0) + sum_yz(1)
     out_ref[...] = final.reshape(2, 8, 1024)
 
     def phi_done(n, _):
@@ -306,15 +363,11 @@
 
     lax.fori_loop(1, 8, phi_done, 0)
 
-    def ex_done(n, _):
-        def one(o, _):
-            ex_copy(n, (sink + o) % 16, sink).wait_send()
-            return 0
-
-        lax.fori_loop(1, 16, one, 0)
-        return 0
-
-    lax.fori_loop(0, PIECES, ex_done, 0)
+    def ex_done(q, _):
+        ex_send(q).wait_send()
+        return 0
+
+    lax.fori_loop(15 * PIECES - WINDOW, 15 * PIECES, ex_done, 0)
 
     def core_done(g, _):
         core_copy(g).wait_send()
@@ -329,7 +382,8 @@
     lax.fori_loop(0, 12, x_done, 0)
 
     def last_done(n, _):
-        last_copy(n).wait_send()
+        last_copy(0, n).wait_send()
+        last_copy(1, n).wait_send()
         return 0
 
     lax.fori_loop(1, 16, last_done, 0)
@@ -361,11 +415,11 @@
             pltpu.VMEM((3, 4, 256, 256), BF16),
             pltpu.VMEM((3, 4, 256, 256), BF16),
             pltpu.VMEM((4, 256, 256), F32),
-            pltpu.VMEM((16, 16, 1024), BF16),
-            pltpu.VMEM((16, 16, 1024), BF16),
+            pltpu.VMEM((2, 16, 16, 512), BF16),
+            pltpu.VMEM((2, 16, 16, 512), BF16),
             dma, dma((8,)), dma((8,)), dma((4, 16)), dma((4, 16)),
             dma((16,)), dma((16,)), dma((3, 4)), dma((3, 4)),
-            dma((16,)), dma((16,)),
+            dma((2, 16)), dma((2, 16)),
         ],
         compiler_params=pltpu.CompilerParams(
             collective_id=0, has_side_effects=True, vmem_limit_bytes=60 * 2**20

time: 96.8 us -> 90.8 us (0.938); the launches traced: 95.1 us -> 90.6 us
  Pallas kernels: 93 us -> 88.5 us
    pallas_call x1, Pallas kernels: 93 us -> 88.5 us  [on_device(): pl.pallas_call(kernel, out_shape=jax.ShapeDtypeStruct((2, 8, 1024), F32),...]
where the time goes in v2:
time: 90.8 us; the launch traced here: 90.6 us
  Pallas kernels  88.5 us (97%)
  local copies, waits for them, and re-layouts  1.47 us (2%)
    pallas_call x1, Pallas kernels, on_device(): pl.pallas_call(kernel, out_shape=jax.ShapeDtypeStruct((2, 8, 1024), F32),...  88.5 us

profile of v2, /device:TPU:1, one launch (start us, length us, event | category | flops | bytes accessed | tf_op | source)
XLA Modules:
  0.0 90.6 jit_solution(1025101476157737370)
XLA Ops:
  0.7 88.5 %shard_map.64 = f32[2,8,1024]{2,1,0:T(8,128)} custom-call(s32[1]{0:T(128)S(6)} %copy.8.momentum, s32[16]{0:T(128)} %owner_slot.1, bf16[4,2,32,256]{3,2,1,0:T(8,128)(2,1)} %bitcast.7, s32[16,16]{1,0:T(8,128)} %bitcast.8, s32[16,16]{1,0:T(8,128)} %bitcast.9, bf16[2,1024,1024]{2,1,0:T(8,128)(2,1)} %bitcast.6), custom_call_target="tpu_custom_call" | custom-call | flops 20000000000 | bytes 8388608 | tf_op jit(solution)/shard_map/pallas_call | solution.py:396
  89.1 1.5 %copy.9 = f32[1,2,8,1024]{3,2,1,0:T(8,128)} copy(f32[1,2,8,1024]{3,2,1,0:T(8,128)} %bitcast.5) | data formatting | bytes 131072

commit v3 on v2

--- a/solution.py
+++ b/solution.py
@@ -9,7 +9,8 @@
 F32 = jnp.float32
 BF16 = jnp.bfloat16
 PIECES = 4
-WINDOW = 24
+AHEAD = 9
+SORTED_FIRST = 4
 
 
 def packed(values, bits):
@@ -26,6 +27,7 @@
 PEERS_Y = packed([p[0] for p in PEERS], 2)
 PEERS_Z = packed([p[1] for p in PEERS], 1)
 PEERS_C = packed([p[2] for p in PEERS], 1)
+SHARES = packed((1, 2, 3, 0), 2)
 
 def iota(shape, dim):
     return lax.broadcasted_iota(jnp.int32, shape, dim)
@@ -48,8 +50,8 @@
 ):
     source = lax.axis_index("src")
     sink = lax.axis_index("snk")
-    zl, xx = source // 4, source % 4
-    yy, zh, core = sink // 4, (sink // 2) % 2, sink % 2
+    zl, xx = source >> 2, source & 3
+    yy, zh, core = sink >> 2, (sink >> 1) & 1, sink & 1
 
     load = pltpu.make_async_copy(tile_hbm, tile, tile_sem)
     load.start()
@@ -60,15 +62,15 @@
         pl.semaphore_signal(barrier, inc=1, device_id=there, device_id_type=MESH)
 
     def greet_source(n, _):
-        greet(((source + n) % 8, sink))
+        greet(((source + n) & 7, sink))
         return 0
 
     def greet_sink(n, _):
-        greet((source, (sink + n) % 16))
+        greet((source, (sink + n) & 15))
         return 0
 
     def greet_other(n, _):
-        greet(((source + 4) % 8, (sink + 2 * n) % 16))
+        greet((source ^ 4, (sink + 2 * n) & 15))
         return 0
 
     lax.fori_loop(1, 8, greet_source, 0)
@@ -76,15 +78,22 @@
     lax.fori_loop(1, 8, greet_other, 0)
 
     row, col = iota((256, 256), 0), iota((256, 256), 1)
-    phi[source] = elementals[momentum[0]]
+    chosen = elementals[momentum[0]].reshape(64, 256)
+    r64, c64 = iota((64, 64), 0), iota((64, 64), 1)
+    wanted = ((r64 >> 3) & 1) * 32 + ((r64 >> 1) & 3) * 8 + (r64 >> 4) * 2 + (r64 & 1)
+    pieces = jnp.where(c64 == wanted, 1.0, 0.0).astype(BF16)
+    phi[source] = dot(pieces, chosen).astype(BF16).reshape(4, 16, 256)
 
     def chip_at(h):
         dy, dz = (CHIPS_Y >> (2 * h)) & 3, (CHIPS_Z >> h) & 1
-        return ((yy + dy) % 4) * 2 + (zh + dz) % 2
+        return ((yy + dy) & 3) * 2 + (zh ^ dz)
+
+    def share(n):
+        return (xx + (SHARES >> (2 * n))) & 3
 
     def peer_at(j):
         dy, dz, dc = (PEERS_Y >> (2 * j)) & 3, (PEERS_Z >> j) & 1, (PEERS_C >> j) & 1
-        return ((yy + dy) % 4) * 4 + ((zh + dz) % 2) * 2 + (core + dc) % 2
+        return ((yy + dy) & 3) * 4 + (zh ^ dz) * 2 + (core ^ dc)
 
     spins = jnp.where(col == (row & 63) * 4 + (row >> 6), 1.0, 0.0).astype(BF16)
 
@@ -102,34 +111,50 @@
 
     pl.semaphore_wait(barrier, 29)
 
-    def phi_copy(n, owner):
+    def phi_copy(n, step):
+        there = (source + step) & 7
         return pltpu.make_async_remote_copy(
-            src_ref=phi.at[owner], dst_ref=phi.at[owner],
-            send_sem=phi_s.at[n], recv_sem=phi_r.at[n],
-            device_id=((source + n) % 8, sink), device_id_type=MESH,
+            src_ref=phi.at[source, (there + (SHARES >> (2 * n))) & 3],
+            dst_ref=phi.at[source, (there + (SHARES >> (2 * n))) & 3],
+            send_sem=phi_s.at[n, step], recv_sem=phi_r.at[n, step],
+            device_id=(there, sink), device_id_type=MESH,
         )
 
-    def phi_start(n, _):
-        phi_copy(n, source).start()
-        return 0
-
-    lax.fori_loop(1, 8, phi_start, 0)
+    def phi_arrival(n, step):
+        owner = (source + 8 - step) & 7
+        return pltpu.make_async_remote_copy(
+            src_ref=phi.at[owner, share(n)], dst_ref=phi.at[owner, share(n)],
+            send_sem=phi_s.at[n, step], recv_sem=phi_r.at[n, step],
+            device_id=(owner, sink), device_id_type=MESH,
+        )
+
+    def phi_start(n):
+        def one(step, _):
+            phi_copy(n, step).start()
+            return 0
+
+        lax.fori_loop(1, 8, one, 0)
+
+    phi_start(0)
     load.wait()
-    lax.fori_loop(0, 8, by_spin, 0)
-
-    t = (xx + 1 + (row >> 6)) & 3
-    wanted = (row & 15) * 16 + ((row >> 5) & 1) * 8 + t * 2 + ((row >> 4) & 1)
-    place = jnp.where(col == wanted, 1.0, 0.0).astype(BF16)
-
-    def phi_wait(n, _):
-        phi_copy(n, (source + 8 - n) % 8).wait_recv()
-        return 0
-
-    lax.fori_loop(1, 8, phi_wait, 0)
-    for part in range(2):
-        whole = jnp.concatenate([phi[q, part] for q in range(8)], axis=0)
-        placed[part * 256:(part + 1) * 256, :] = dot(place, whole).astype(BF16)
-
+    lax.fori_loop(0, SORTED_FIRST, by_spin, 0)
+
+    r128, c128 = iota((128, 128), 0), iota((128, 128), 1)
+    wanted = ((r128 >> 1) & 7) * 16 + (r128 >> 6) * 8 + (r128 & 1) * 4 + ((r128 >> 5) & 1) * 2 + ((r128 >> 4) & 1)
+    place = jnp.where(c128 == wanted, 1.0, 0.0).astype(BF16)
+
+    def phi_place(n):
+        def wait(step, _):
+            phi_arrival(n, step).wait_recv()
+            return 0
+
+        lax.fori_loop(1, 8, wait, 0)
+        whole = jnp.concatenate([phi[q, share(n)] for q in range(8)], axis=0)
+        placed[n] = dot(place, whole).astype(BF16)
+
+    for n in range(1, PIECES):
+        phi_start(n)
+    phi_place(0)
     low_lanes = iota((256, 128), 1) < 64
 
     def ex_copy(n, dest, origin):
@@ -139,44 +164,71 @@
             device_id=(source, dest), device_id_type=MESH,
         )
 
-    def columns(chip, a):
-        both = dot(placed[...], right[chip, a])
-        real = both[:256, :128] - both[256:, 128:]
-        imag = both[:256, 128:] + both[256:, :128]
-        low = jnp.where(low_lanes, real, pltpu.roll(imag, 64, 1)).astype(BF16)
-        high = jnp.where(low_lanes, pltpu.roll(real, 64, 1), imag).astype(BF16)
+    def columns(chip, a, start, stop):
+        count = stop - start
+        both = dot(placed[start:stop].reshape(count * 128, 256), right[chip, a])
+        both = both.reshape(count, 2, 64, 256)
+        real = (both[:, 0, :, :128] - both[:, 1, :, 128:]).reshape(count * 64, 128)
+        imag = (both[:, 0, :, 128:] + both[:, 1, :, :128]).reshape(count * 64, 128)
+        left = iota((count * 64, 128), 1) < 64
+        low = jnp.where(left, real, pltpu.roll(imag, 64, 1)).astype(BF16)
+        high = jnp.where(left, pltpu.roll(real, 64, 1), imag).astype(BF16)
         return low, high
 
-    def dress(h, _):
+    def dress_remote(h, start, stop):
         chip = chip_at(h)
         for a in range(4):
-            low, high = columns(chip, a)
-            for n in range(PIECES):
-                sent[n, 2 * chip, a * 64:(a + 1) * 64] = low[n * 64:(n + 1) * 64]
-                sent[n, 2 * chip + 1, a * 64:(a + 1) * 64] = high[n * 64:(n + 1) * 64]
+            low, high = columns(chip, a, start, stop)
+            for n in range(start, stop):
+                rows = slice((n - start) * 64, (n - start + 1) * 64)
+                sent[n, 2 * chip, a * 64:(a + 1) * 64] = low[rows]
+                sent[n, 2 * chip + 1, a * 64:(a + 1) * 64] = high[rows]
+
+    partner = sink + 1 - 2 * core
+
+    def dress_own(start, stop):
+        for a in range(4):
+            low, high = columns(yy * 2 + zh, a, start, stop)
+            mine = jnp.where(core == 0, low, high)
+            theirs = jnp.where(core == 0, high, low)
+            for n in range(start, stop):
+                rows = slice((n - start) * 64, (n - start + 1) * 64)
+                held[n, sink, a * 64:(a + 1) * 64] = mine[rows]
+                sent[n, partner, a * 64:(a + 1) * 64] = theirs[rows]
+
+    def dress_first(h, _):
+        chip = chip_at(h)
+        dress_remote(h, 0, 1)
         ex_copy(0, 2 * chip, sink).start()
         ex_copy(0, 2 * chip + 1, sink).start()
-        return 0
-
-    lax.fori_loop(0, 7, dress, 0)
-    partner = sink + 1 - 2 * core
-    for a in range(4):
-        low, high = columns(yy * 2 + zh, a)
-        mine = jnp.where(core == 0, low, high)
-        theirs = jnp.where(core == 0, high, low)
-        for n in range(PIECES):
-            held[n, sink, a * 64:(a + 1) * 64] = mine[n * 64:(n + 1) * 64]
-            sent[n, partner, a * 64:(a + 1) * 64] = theirs[n * 64:(n + 1) * 64]
+
+        @pl.when(h + SORTED_FIRST < 8)
+        def _():
+            by_spin(h + SORTED_FIRST, 0)
+
+        return 0
+
+    lax.fori_loop(0, 7, dress_first, 0)
+    dress_own(0, 1)
     ex_copy(0, partner, sink).start()
-
-    def ex_send(q):
-        return ex_copy(q // 15, peer_at(q % 15), sink)
-
-    def ex_start(q, _):
-        ex_send(q).start()
-        return 0
-
-    lax.fori_loop(15, WINDOW, ex_start, 0)
+    for n in range(1, PIECES):
+        phi_place(n)
+
+    def dress_rest(h, _):
+        dress_remote(h, 1, PIECES)
+        return 0
+
+    lax.fori_loop(0, 7, dress_rest, 0)
+    dress_own(1, PIECES)
+
+    def ex_send(n, j):
+        return ex_copy(n, peer_at(j), sink)
+
+    def ex_start(j, _):
+        ex_send(1, j).start()
+        return 0
+
+    lax.fori_loop(0, AHEAD, ex_start, 0)
 
     position = jnp.zeros((16, 16), jnp.int32)
     for node in range(16):
@@ -195,7 +247,7 @@
     r, lane = iota((256, 1024), 0), iota((256, 1024), 1)
     target = (r & 15) * 64 + ((r >> 5) & 1) * 32 + ((r >> 4) & 1) * 4 + (r >> 6)
     for m in range(4):
-        t = (xx + 4 - m) % 4
+        t = share(3 - m)
         lane_order[m * 256:(m + 1) * 256] = jnp.where(lane == target + t * 8, 1.0, 0.0).astype(BF16)
 
     def core_copy(g):
@@ -209,13 +261,13 @@
         return pltpu.make_async_remote_copy(
             src_ref=x_out.at[ni, tj], dst_ref=x_in.at[ni, tj],
             send_sem=x_s.at[ni, tj], recv_sem=x_r.at[ni, tj],
-            device_id=(zl * 4 + (xx + 1 + ni) % 4, sink), device_id_type=MESH,
+            device_id=(zl * 4 + share(ni), sink), device_id_type=MESH,
         )
 
     def settle(g, ni, nj):
         core_copy(g).wait_recv()
         total = kept[g] + core_in[g].astype(F32)
-        tj = (xx + 1 + nj) % 4
+        tj = share(nj)
 
         @pl.when(ni < 3)
         def _():
@@ -226,26 +278,29 @@
         def _():
             own_sum[tj] = total
 
-    def block(number, ni, nj):
+    def block(number, ni, nj, beside=()):
         side = jnp.concatenate([held[nj, r] for r in range(16)], axis=1)
         product = dot_nt(factor[ni], side)
+        for pairing in beside:
+            collect(nj, pairing)
         kept[number] = product[:256]
         core_out[number] = product[256:].astype(BF16)
         core_copy(number).start()
 
     def arrive(n):
-        def one(o, _):
-            ex_copy(n, sink, (sink + o) % 16).wait_recv()
-            q = n * 15 + o - 1 + WINDOW
-
-            @pl.when(q < 15 * PIECES)
+        def one(j, _):
+            ex_copy(n, sink, (sink + j + 1) & 15).wait_recv()
+            over = jnp.where(j + AHEAD < 15, 0, 1)
+            later, peer = n + 1 + over, j + AHEAD - 15 * over
+
+            @pl.when(later < PIECES)
             def _():
-                ex_send(q - WINDOW).wait_send()
-                ex_send(q).start()
-
-            return 0
-
-        lax.fori_loop(1, 16, one, 0)
+                ex_send(n, j).wait_send()
+                ex_send(later, peer).start()
+
+            return 0
+
+        lax.fori_loop(0, 15, one, 0)
 
     def earlier_blocks(n, base):
         def earlier(m, _):
@@ -259,27 +314,27 @@
 
         lax.fori_loop(0, n, earlier, 0)
 
-    def collect_piece(n, halfway=None):
-        def collect(pairing, _):
-            first = pl.ds(pl.multiple_of(pairing * 32, 32), 16)
-            second = pl.ds(pl.multiple_of(pairing * 32 + 16, 16), 16)
-            pair = [held[n, :, first, :].reshape(256, 128), held[n, :, second, :].reshape(256, 128)]
-            sums = dot(select[...], jnp.concatenate(pair, axis=1))
-            for k in range(2):
-                plain = sums[:, k * 128:(k + 1) * 128]
-                turned = pltpu.roll(plain, 64, 1)
-                turned = jnp.where(low_lanes, turned, -turned)
-                both = jnp.stack([plain.reshape(32, 8, 128), turned.reshape(32, 8, 128)], axis=1).astype(BF16)
-                for r in range(16):
-                    for c in range(2):
-                        rows = pl.ds(pl.multiple_of(((core + c) % 2) * 256 + pairing * 32 + k * 16, 16), 16)
-                        factor[n, rows, r * 128:(r + 1) * 128] = both[2 * r + c].reshape(16, 128)
-            return 0
-
-        lax.fori_loop(0, 4, collect, 0)
-        if halfway:
-            halfway()
-        lax.fori_loop(4, 8, collect, 0)
+    def collect(n, pairing):
+        first = pl.ds(pl.multiple_of(pairing * 32, 32), 16)
+        second = pl.ds(pl.multiple_of(pairing * 32 + 16, 16), 16)
+        pair = [held[n, :, first, :].reshape(256, 128), held[n, :, second, :].reshape(256, 128)]
+        sums = dot(select[...], jnp.concatenate(pair, axis=1))
+        for k in range(2):
+            plain = sums[:, k * 128:(k + 1) * 128]
+            turned = pltpu.roll(plain, 64, 1)
+            turned = jnp.where(low_lanes, turned, -turned)
+            both = jnp.stack([plain.reshape(32, 8, 128), turned.reshape(32, 8, 128)], axis=1).astype(BF16)
+            for r in range(16):
+                for c in range(2):
+                    rows = pl.ds(pl.multiple_of((core ^ c) * 256 + pairing * 32 + k * 16, 16), 16)
+                    factor[n, rows, r * 128:(r + 1) * 128] = both[2 * r + c].reshape(16, 128)
+
+    def collect_piece(n):
+        def one(pairing, _):
+            collect(n, pairing)
+            return 0
+
+        lax.fori_loop(0, 8, one, 0)
 
     def later_blocks(n, base, start, stop):
         def later(m, _):
@@ -294,16 +349,16 @@
         lax.fori_loop(start, stop, later, 0)
 
     def last_copy(side, n):
-        there = (mine + n) % 16
+        there = (mine + n) & 15
         return pltpu.make_async_remote_copy(
             src_ref=last_out.at[side, there], dst_ref=last_in.at[side, n],
             send_sem=last_s.at[side, n], recv_sem=last_r.at[side, n],
-            device_id=((there % 2) * 4 + xx, (there // 2) * 2 + core), device_id_type=MESH,
+            device_id=((there & 1) * 4 + xx, (there >> 1) * 2 + core), device_id_type=MESH,
         )
 
     def sum_x(side):
         for k in range(2):
-            tj = (xx + 4 - 2 * side - k) % 4
+            tj = share(3 - 2 * side - k)
             summed = own_sum[tj]
             for ni in range(3):
                 x_copy(ni, tj).wait_recv()
@@ -347,9 +402,14 @@
 
     lax.fori_loop(0, 3, piece, 0)
     arrive(3)
-    earlier_blocks(3, 9)
-    collect_piece(3, lambda: settle(11, 2, 3))
-    later_blocks(3, 12, 0, 3)
+    block(9, 0, 3, (0, 1, 2))
+    block(10, 1, 3, (3, 4, 5))
+    settle(9, 0, 3)
+    block(11, 2, 3, (6, 7))
+    settle(10, 1, 3)
+    block(12, 3, 3)
+    settle(11, 2, 3)
+    later_blocks(3, 12, 1, 3)
     sum_x(0)
     later_blocks(3, 12, 3, 4)
     settle(15, 3, 0)
@@ -358,16 +418,22 @@
     out_ref[...] = final.reshape(2, 8, 1024)
 
     def phi_done(n, _):
-        phi_copy(n, source).wait_send()
-        return 0
-
-    lax.fori_loop(1, 8, phi_done, 0)
-
-    def ex_done(q, _):
-        ex_send(q).wait_send()
-        return 0
-
-    lax.fori_loop(15 * PIECES - WINDOW, 15 * PIECES, ex_done, 0)
+        for step in range(1, 8):
+            phi_copy(n, step).wait_send()
+        return 0
+
+    lax.fori_loop(0, PIECES, phi_done, 0)
+
+    def ex_done(j, _):
+        ex_send(3, j).wait_send()
+
+        @pl.when(j >= 15 - AHEAD)
+        def _():
+            ex_send(2, j).wait_send()
+
+        return 0
+
+    lax.fori_loop(0, 15, ex_done, 0)
 
     def core_done(g, _):
         core_copy(g).wait_send()
@@ -401,8 +467,8 @@
         scratch_shapes=[
             pltpu.VMEM((2, 1024, 1024), BF16),
             pltpu.VMEM((8, 4, 256, 256), BF16),
-            pltpu.VMEM((8, 2, 32, 256), BF16),
-            pltpu.VMEM((512, 256), BF16),
+            pltpu.VMEM((8, 4, 16, 256), BF16),
+            pltpu.VMEM((4, 128, 256), BF16),
             pltpu.VMEM((256, 256), BF16),
             pltpu.VMEM((256, 256), BF16),
             pltpu.VMEM((1024, 1024), BF16),
@@ -417,7 +483,7 @@
             pltpu.VMEM((4, 256, 256), F32),
             pltpu.VMEM((2, 16, 16, 512), BF16),
             pltpu.VMEM((2, 16, 16, 512), BF16),
-            dma, dma((8,)), dma((8,)), dma((4, 16)), dma((4, 16)),
+            dma, dma((4, 8)), dma((4, 8)), dma((4, 16)), dma((4, 16)),
             dma((16,)), dma((16,)), dma((3, 4)), dma((3, 4)),
             dma((2, 16)), dma((2, 16)),
         ],

time: 90.8 us -> 89.4 us (0.985)
  Pallas kernels: 88.5 us -> 87.1 us
    pallas_call x1, Pallas kernels: 88.5 us -> 87.1 us  [on_device(): pl.pallas_call(kernel, out_shape=jax.ShapeDtypeStruct((2, 8, 1024), F32),...]
where the time goes in v3:
time: 89.4 us; the launch traced here: 89.3 us
  Pallas kernels  87.1 us (97%)
  local copies, waits for them, and re-layouts  1.47 us (2%)
    pallas_call x1, Pallas kernels, on_device(): pl.pallas_call(kernel, out_shape=jax.ShapeDtypeStruct((2, 8, 1024), F32),...  87.1 us

profile of v3, /device:TPU:1, one launch (start us, length us, event | category | flops | bytes accessed | tf_op | source)
XLA Modules:
  0.0 89.3 jit_solution(5244061362908800812)
XLA Ops:
  0.7 87.1 %shard_map.64 = f32[2,8,1024]{2,1,0:T(8,128)} custom-call(s32[1]{0:T(128)S(6)} %copy.8.momentum, s32[16]{0:T(128)} %owner_slot.1, bf16[4,2,32,256]{3,2,1,0:T(8,128)(2,1)} %bitcast.7, s32[16,16]{1,0:T(8,128)} %bitcast.8, s32[16,16]{1,0:T(8,128)} %bitcast.9, bf16[2,1024,1024]{2,1,0:T(8,128)(2,1)} %bitcast.6), custom_call_target="tpu_custom_call" | custom-call | flops 20000000000 | bytes 8388608 | tf_op jit(solution)/shard_map/pallas_call | solution.py:462
  87.8 1.5 %copy.9 = f32[1,2,8,1024]{3,2,1,0:T(8,128)} copy(f32[1,2,8,1024]{3,2,1,0:T(8,128)} %bitcast.5) | data formatting | bytes 131072

commit v4 on v3

--- a/solution.py
+++ b/solution.py
@@ -42,20 +42,18 @@
 
 
 def kernel(
-    momentum, owner_slot, elementals, routes, node_of, tile_hbm, out_ref,
+    momentum_in, owner_slot_in, elementals_in, routes_in, node_of_in, tile_in, out_ref,
+    momentum, owner_slot, elementals, routes, node_of,
     tile, right, phi, placed, select, rows_order, lane_order,
     sent, held, factor, kept, core_out, core_in,
     x_out, x_in, own_sum, last_out, last_in,
-    tile_sem, phi_s, phi_r, ex_s, ex_r, core_s, core_r, x_s, x_r, last_s, last_r,
+    load_sem, phi_s, phi_r, ex_s, ex_r, core_s, core_r, x_s, x_r, last_s, last_r,
 ):
     source = lax.axis_index("src")
     sink = lax.axis_index("snk")
     zl, xx = source >> 2, source & 3
     yy, zh, core = sink >> 2, (sink >> 1) & 1, sink & 1
 
-    load = pltpu.make_async_copy(tile_hbm, tile, tile_sem)
-    load.start()
-
     barrier = pltpu.get_barrier_semaphore()
 
     def greet(there):
@@ -77,7 +75,20 @@
     lax.fori_loop(1, 16, greet_sink, 0)
     lax.fori_loop(1, 8, greet_other, 0)
 
+    loads = [
+        pltpu.make_async_copy(momentum_in, momentum, load_sem.at[0]),
+        pltpu.make_async_copy(elementals_in, elementals, load_sem.at[1]),
+        pltpu.make_async_copy(tile_in, tile, load_sem.at[2]),
+        pltpu.make_async_copy(routes_in, routes, load_sem.at[3]),
+        pltpu.make_async_copy(node_of_in, node_of, load_sem.at[4]),
+        pltpu.make_async_copy(owner_slot_in, owner_slot, load_sem.at[5]),
+    ]
+    for load in loads:
+        load.start()
+
     row, col = iota((256, 256), 0), iota((256, 256), 1)
+    loads[0].wait()
+    loads[1].wait()
     chosen = elementals[momentum[0]].reshape(64, 256)
     r64, c64 = iota((64, 64), 0), iota((64, 64), 1)
     wanted = ((r64 >> 3) & 1) * 32 + ((r64 >> 1) & 3) * 8 + (r64 >> 4) * 2 + (r64 & 1)
@@ -136,7 +147,7 @@
         lax.fori_loop(1, 8, one, 0)
 
     phi_start(0)
-    load.wait()
+    loads[2].wait()
     lax.fori_loop(0, SORTED_FIRST, by_spin, 0)
 
     r128, c128 = iota((128, 128), 0), iota((128, 128), 1)
@@ -230,6 +241,8 @@
 
     lax.fori_loop(0, AHEAD, ex_start, 0)
 
+    for load in loads[3:]:
+        load.wait()
     position = jnp.zeros((16, 16), jnp.int32)
     for node in range(16):
         position = position + jnp.where(node_of[...] == node, owner_slot[node], 0)
@@ -457,14 +470,18 @@
 
 def on_device(perambulator, elementals, momentum, routes, node_of, owner_slot):
     vmem = pl.BlockSpec(memory_space=pltpu.VMEM)
-    smem = pl.BlockSpec(memory_space=pltpu.SMEM)
     dma = pltpu.SemaphoreType.DMA
     out = pl.pallas_call(
         kernel,
         out_shape=jax.ShapeDtypeStruct((2, 8, 1024), F32),
-        in_specs=[smem, smem, vmem, vmem, vmem, pl.BlockSpec(memory_space=pl.ANY)],
+        in_specs=[pl.BlockSpec(memory_space=pl.ANY)] * 6,
         out_specs=vmem,
         scratch_shapes=[
+            pltpu.SMEM((1,), jnp.int32),
+            pltpu.SMEM((16,), jnp.int32),
+            pltpu.VMEM((4, 2, 32, 256), BF16),
+            pltpu.VMEM((16, 16), jnp.int32),
+            pltpu.VMEM((16, 16), jnp.int32),
             pltpu.VMEM((2, 1024, 1024), BF16),
             pltpu.VMEM((8, 4, 256, 256), BF16),
             pltpu.VMEM((8, 4, 16, 256), BF16),
@@ -483,7 +500,7 @@
             pltpu.VMEM((4, 256, 256), F32),
             pltpu.VMEM((2, 16, 16, 512), BF16),
             pltpu.VMEM((2, 16, 16, 512), BF16),
-            dma, dma((4, 8)), dma((4, 8)), dma((4, 16)), dma((4, 16)),
+            dma((6,)), dma((4, 8)), dma((4, 8)), dma((4, 16)), dma((4, 16)),
             dma((16,)), dma((16,)), dma((3, 4)), dma((3, 4)),
             dma((2, 16)), dma((2, 16)),
         ],

time: 89.4 us -> 88.6 us (level)
  no operation moved by 1% of the time
where the time goes in v4:
time: 88.6 us; the launch traced here: 88.4 us
  Pallas kernels  86.3 us (97%)
  local copies, waits for them, and re-layouts  1.47 us (2%)
    pallas_call x1, Pallas kernels, on_device(): pl.pallas_call(kernel, out_shape=jax.ShapeDtypeStruct((2, 8, 1024), F32),...  86.3 us

profile of v4, /device:TPU:1, one launch (start us, length us, event | category | flops | bytes accessed | tf_op | source)
XLA Modules:
  0.0 88.4 jit_solution(11683155017423105098)
XLA Ops:
  0.7 86.3 %shard_map.64 = f32[2,8,1024]{2,1,0:T(8,128)} custom-call(s32[1]{0:T(128)S(6)} %copy.8.momentum_in, s32[16]{0:T(128)} %owner_slot_in.1, bf16[4,2,32,256]{3,2,1,0:T(8,128)(2,1)} %bitcast.7, s32[16,16]{1,0:T(8,128)} %bitcast.8, s32[16,16]{1,0:T(8,128)} %bitcast.9, bf16[2,1024,1024]{2,1,0:T(8,128)(2,1)} %bitcast.6), custom_call_target="tpu_custom_call" | custom-call | flops 20000000000 | bytes 8388608 | tf_op jit(solution)/shard_map/pallas_call | solution.py:474
  86.9 1.5 %copy.9 = f32[1,2,8,1024]{3,2,1,0:T(8,128)} copy(f32[1,2,8,1024]{3,2,1,0:T(8,128)} %bitcast.5) | data formatting | bytes 131072

commit v5 on v4

--- a/solution.py
+++ b/solution.py
@@ -342,12 +342,12 @@
                     rows = pl.ds(pl.multiple_of((core ^ c) * 256 + pairing * 32 + k * 16, 16), 16)
                     factor[n, rows, r * 128:(r + 1) * 128] = both[2 * r + c].reshape(16, 128)
 
-    def collect_piece(n):
+    def collect_some(n, start, stop):
         def one(pairing, _):
             collect(n, pairing)
             return 0
 
-        lax.fori_loop(0, 8, one, 0)
+        lax.fori_loop(start, stop, one, 0)
 
     def later_blocks(n, base, start, stop):
         def later(m, _):
@@ -402,7 +402,7 @@
 
     def piece(n, _):
         arrive(n)
-        collect_piece(n)
+        collect_some(n, 0, 8)
         later_blocks(n, n * n, 0, n + 1)
         earlier_blocks(n, n * n + n + 1)
         settle(n * n + n, n, 0)
@@ -415,13 +415,15 @@
 
     lax.fori_loop(0, 3, piece, 0)
     arrive(3)
-    block(9, 0, 3, (0, 1, 2))
-    block(10, 1, 3, (3, 4, 5))
+    block(9, 0, 3)
+    block(10, 1, 3)
     settle(9, 0, 3)
-    block(11, 2, 3, (6, 7))
+    block(11, 2, 3)
     settle(10, 1, 3)
+    collect_some(3, 0, 3)
+    settle(11, 2, 3)
+    collect_some(3, 3, 8)
     block(12, 3, 3)
-    settle(11, 2, 3)
     later_blocks(3, 12, 1, 3)
     sum_x(0)
     later_blocks(3, 12, 3, 4)

time: 88.6 us -> 88.6 us (level)
  no operation moved by 1% of the time
where the time goes in v5:
time: 88.6 us; the launch traced here: 88.4 us
  Pallas kernels  86.3 us (97%)
  local copies, waits for them, and re-layouts  1.47 us (2%)
    pallas_call x1, Pallas kernels, on_device(): pl.pallas_call(kernel, out_shape=jax.ShapeDtypeStruct((2, 8, 1024), F32),...  86.3 us

profile of v5, /device:TPU:1, one launch (start us, length us, event | category | flops | bytes accessed | tf_op | source)
XLA Modules:
  0.0 88.4 jit_solution(6758426229485696508)
XLA Ops:
  0.7 86.3 %shard_map.64 = f32[2,8,1024]{2,1,0:T(8,128)} custom-call(s32[1]{0:T(128)S(6)} %copy.8.momentum_in, s32[16]{0:T(128)} %owner_slot_in.1, bf16[4,2,32,256]{3,2,1,0:T(8,128)(2,1)} %bitcast.7, s32[16,16]{1,0:T(8,128)} %bitcast.8, s32[16,16]{1,0:T(8,128)} %bitcast.9, bf16[2,1024,1024]{2,1,0:T(8,128)(2,1)} %bitcast.6), custom_call_target="tpu_custom_call" | custom-call | flops 20000000000 | bytes 8388608 | tf_op jit(solution)/shard_map/pallas_call | solution.py:476
  86.9 1.5 %copy.9 = f32[1,2,8,1024]{3,2,1,0:T(8,128)} copy(f32[1,2,8,1024]{3,2,1,0:T(8,128)} %bitcast.5) | data formatting | bytes 131072
